TPU v7x, 128 devices: a whole 4x4x4 slice. The times are simulated.
128 devices in a mesh: ctx: 16 (over z_lo, y, core), tp: 8 (over x, z_hi).
Axes of the slice: x: 4, y: 4, z: 4 (z_hi: 2, z_lo: 2; z = z_hi * 2 + z_lo), core: 2. Of those that a mesh axis runs over, the one named last changes fastest.
Arguments:
- tokens: bfloat16 [16384, 4096], P('ctx', 'tp'), may hold values from -6 to 6
- grad_out: bfloat16 [16384, 4096], P('ctx', 'tp'), may hold values from -1.1953125 to 1.1953125
- expert_ids: int32 [16384, 2], P(('ctx', 'tp')), may hold values from 0 to 63, all different within a row; in each aligned block of 128 rows (0 to 127, 128 to 255, ...) at most 6 rows name the same one
- gates: float32 [16384, 2], P(('ctx', 'tp')), may hold values from 0.1 to 1
- w_gate: bfloat16 [128, 4096, 768], P(('ctx', 'tp')), may hold values from -0.09375 to 0.09375
- w_up: bfloat16 [128, 4096, 768], P(('ctx', 'tp')), may hold values from -0.09375 to 0.09375
- w_down: bfloat16 [128, 768, 4096], P(('ctx', 'tp')), may hold values from -0.15625 to 0.15625
Outputs:
- grad_tokens: bfloat16 [16384, 4096], P('ctx', 'tp')
- grad_gates: float32 [16384, 2], P(('ctx', 'tp'))
Inputs may be any that keep to these rules, and one draw needn't show every extreme that they name: `expert_ids`: in the 128 rows of one device no expert is named by more than 6 rows, a bound that some block reaches; the 2 experts of a row differ; every expert is named somewhere.
All inputs are finite; a program needn't handle non-finite values.
Results may differ from a plain program's by a relative error of at most 0.015.
Values may be sent and summed in bfloat16 or wider, within the bound.
A program may use at most 192 MiB of HBM per device.

v0:
```python
import functools

import jax
import jax.numpy as jnp
from jax import lax
from jax.experimental import pallas as pl
from jax.experimental.pallas import tpu as pltpu
from jax.sharding import PartitionSpec as P

MESH = pl.DeviceIdType.MESH
F32 = jnp.float32
BF16 = jnp.bfloat16

CAP = 6
BLK = 48
CHUNK = 384
ROWS = 1536
TOK = 1024
SH = 512
HID = 768
WIDTH = 4096


def dot(left, right):
    return jnp.dot(left, right, preferred_element_type=F32)


def dot_last(left, right):
    return lax.dot_general(left, right, (((1,), (1,)), ((), ())), preferred_element_type=F32)


def kernel(
    pack, tok, dy, wg_hbm, wu_hbm, wd_hbm,
    out, vout,
    wg, wu, wd, xrow, yrow, stage, xg, dyz, yg, back, ret,
    pre, bh, posb, post, pgs, pgl, gs, gb,
    w_sem, pos_s, pos_r, z_s, z_r, a1_s, a1x_r, a1p_r, a2_s, a2_r,
    b2_s, b2_r, r1_s, r1_r, r2_s, r2_r, g1_s, g1_r, g2_s, g2_r,
):
    ctx, tp = lax.axis_index("ctx"), lax.axis_index("tp")
    zl, yc, x, zh = ctx // 8, ctx % 8, tp // 2, tp % 2
    ozl, ozh = 1 - zl, 1 - zh
    plane = zl * 2 + zh
    q = x * 8 + yc

    def dev(zl_, yc_, x_, zh_):
        return (zl_ * 8 + yc_, x_ * 2 + zh_)

    def plane_of(m):
        return (zl + ((m + 1) // 2) % 2) % 2, (zh + m // 2) % 2

    def peer(m):
        zl_, zh_ = plane_of(m)
        return dev(zl_, yc, x, zh_)

    def near_first(i):
        return i + (i // 2) * (5 - 2 * i)

    def rows(n):
        return pl.ds(pl.multiple_of(n * BLK, BLK), BLK)

    def chunk(n):
        return pl.ds(pl.multiple_of(n * CHUNK, CHUNK), CHUNK)

    def send(src, dst, s_sem, r_sem, to):
        pltpu.make_async_remote_copy(
            src_ref=src, dst_ref=dst, send_sem=s_sem, recv_sem=r_sem,
            device_id=to, device_id_type=MESH,
        ).start()

    def wait(ref, sem):
        pltpu.make_async_copy(ref, ref, sem).wait()

    bar = pltpu.get_barrier_semaphore()

    def greet_plane(i, c):
        to = dev(zl, (yc + i % 8) % 8, (x + i // 8) % 4, zh)
        pl.semaphore_signal(bar, inc=1, device_id=to, device_id_type=MESH)
        return c

    def greet_other(i, c):
        zl_, zh_ = plane_of(1 + i // 4)
        to = dev(zl_, yc, (x + i % 4) % 4, zh_)
        pl.semaphore_signal(bar, inc=1, device_id=to, device_id_type=MESH)
        return c

    lax.fori_loop(1, 32, greet_plane, 0)
    lax.fori_loop(0, 12, greet_other, 0)
    loads = [
        pltpu.make_async_copy(wg_hbm, wg, w_sem.at[0]),
        pltpu.make_async_copy(wu_hbm, wu, w_sem.at[1]),
        pltpu.make_async_copy(wd_hbm, wd, w_sem.at[2]),
    ]
    for load in loads:
        load.start()
    pl.semaphore_wait(bar, 43)

    mine = posb.at[zl * 8 + tp]
    pltpu.make_async_copy(pack, mine, pos_r).start()

    def send_pos(i, c):
        to = dev((zl + i // 8) % 2, yc, (x + (i // 2) % 4) % 4, (zh + i % 2) % 2)
        send(pack, mine, pos_s, pos_r, to)
        return c

    lax.fori_loop(1, 16, send_pos, 0)
    for m in (1, 2, 3):
        send(dy, dyz.at[m - 1], z_s.at[m - 1], z_r.at[m - 1], peer(m))
    wait(posb, pos_r)

    def select(zl_, c):
        place = (lax.broadcasted_iota(jnp.int32, (CHUNK, 128), 0) + c * CHUNK).astype(F32)
        parts = []
        for n in range(8):
            tile = posb[zl_ * 8 + n]
            hit = (place == tile[0:1]) | (place == tile[1:2])
            parts.append(jnp.where(hit, 1.0, 0.0).astype(BF16))
        return jnp.concatenate(parts, axis=1)

    def spread(i, src_of, dst_of, s_sem, r_sem, xd, dx):
        def one(j, c):
            ycd = (yc + j) % 8
            src, dst = src_of(rows(xd * 8 + ycd)), dst_of(rows(q))
            own = dx * 8 + j == 0

            @pl.when(own)
            def _():
                pltpu.make_async_copy(src, dst, r_sem).start()

            @pl.when(jnp.logical_not(own))
            def _():
                send(src, dst, s_sem, r_sem, dev(zl, ycd, xd, zh))

            return c

        lax.fori_loop(0, 8, one, 0)

    def x_out(i, c):
        dx = near_first(i)
        xd = (x + dx) % 4
        for s in (0, 1):
            zt = (zl + s) % 2
            xg[s, chunk(xd), :] = dot(select(zl, zt * 4 + xd), tok[...]).astype(BF16)
        spread(i, lambda r: xg.at[1, r], lambda r: stage.at[r], a1_s.at[1], a1p_r.at[dx], xd, dx)
        spread(i, lambda r: xg.at[0, r], lambda r: xrow.at[plane, r], a1_s.at[0], a1x_r.at[dx], xd, dx)
        return c

    def y_out(m):
        zl_, zh_ = plane_of(m)
        slot = m % 2
        src = dy if m == 0 else dyz.at[m - 1]
        if m > 0:
            wait(dyz.at[m - 1], z_r.at[m - 1])
        if m > 1:
            wait(yg.at[slot, pl.ds(0, ROWS - BLK)], b2_s.at[m - 2])
            old_zl, old_zh = plane_of(m - 2)
            wait(yrow.at[old_zl * 2 + old_zh, chunk(x)], b2_r.at[m - 2, 0])

        def step(i, c):
            dx = near_first(i)
            xd = (x + dx) % 4
            yg[slot, chunk(xd), :] = dot(select(zl_, zl * 4 + xd), src[...]).astype(BF16)
            spread(
                i, lambda r: yg.at[slot, r], lambda r: yrow.at[zl_ * 2 + zh_, r],
                b2_s.at[m], b2_r.at[m, dx], xd, dx,
            )
            return c

        lax.fori_loop(0, 4, step, 0)

    def forward(dx):
        part = chunk((x + 4 - dx) % 4)
        wait(stage.at[part], a1p_r.at[dx])
        for m in (1, 2):
            send(stage.at[part], xrow.at[plane, part], a2_s.at[m - 1], a2_r.at[m - 1, dx], peer(m))
        wait(xrow.at[plane, part], a1x_r.at[dx])
        send(xrow.at[plane, part], xrow.at[plane, part], a2_s.at[2], a2_r.at[2, dx], peer(3))

    lax.fori_loop(0, 4, x_out, 0)
    y_out(0)
    forward(0)
    forward(1)
    y_out(1)
    forward(3)
    y_out(2)
    forward(2)
    y_out(3)

    pre[...] = jnp.zeros_like(pre)
    bh[...] = jnp.zeros_like(bh)
    for load in loads:
        load.wait()

    def shard(n):
        return pl.ds(pl.multiple_of(n * SH, SH), SH)

    def consume(n, c):
        dx, m = near_first(n // 4), n % 4
        xs = (x + 4 - dx) % 4
        zl_, zh_ = plane_of(m)
        src = xrow.at[zl_ * 2 + zh_, chunk(xs)]

        @pl.when(m > 0)
        def _():
            wait(src, a2_r.at[m - 1, dx])

        part = shard(xs * 2 + zh_)
        pre[zl_] += dot(src[...], wg[part, :])
        pre[2 + zl_] += dot(src[...], wu[part, :])

        dx, m = near_first(n % 4), n // 4
        xs = (x + 4 - dx) % 4
        zl_, zh_ = plane_of(m)
        src = yrow.at[zl_ * 2 + zh_, chunk(xs)]

        @pl.when(jnp.logical_or(m > 1, dx > 0))
        def _():
            wait(src, b2_r.at[m, dx])

        bh[zl_] += dot_last(src[...], wd[:, shard(xs * 2 + zh_)])
        return c

    lax.fori_loop(0, 16, consume, 0)

    def inner(n, c):
        s, part = n // 8, rows(n % 8)
        av, bv, hv = pre[s, part, :], pre[2 + s, part, :], bh[s, part, :]
        sigma = 1.0 / (1.0 + jnp.exp(-av))
        active = av * sigma
        hidden = (active * bv).astype(BF16).astype(F32)
        wd[rows(n), 0:HID] = (hv * bv * sigma * (1.0 + av * (1.0 - sigma))).astype(BF16)
        wd[rows(n), HID : 2 * HID] = (hv * active).astype(BF16)
        gate = jnp.sum(hidden * hv, axis=1, keepdims=True)
        diag = lax.broadcasted_iota(jnp.int32, (BLK, 128), 0) == lax.broadcasted_iota(
            jnp.int32, (BLK, 128), 1
        )
        pgs[s, pl.ds(n % 8, 1), :] = jnp.sum(jnp.where(diag, gate, 0.0), axis=0, keepdims=True)
        return c

    lax.fori_loop(0, 16, inner, 0)
    for m in (1, 2, 3):
        send(pgs.at[plane_of(m)[0]], pgl.at[m - 1], g1_s.at[m - 1], g1_r.at[m - 1], peer(m))

    for m in (0, 1, 2):
        wait(xrow.at[0], a2_s.at[m])
    for s in (0, 1):
        wait(xg.at[s, pl.ds(0, ROWS - BLK)], a1_s.at[s])

    def x_back(i, c):
        dx = near_first(3 - i)
        xs = (x + dx) % 4
        part = chunk(xs)
        for m in (1, 2, 3, 0):
            zl_, zh_ = plane_of(m)
            piece = shard(xs * 2 + zh_)
            val = dot_last(wd[chunk(zl_), 0:HID], wg[piece, :])
            val += dot_last(wd[chunk(zl_), HID : 2 * HID], wu[piece, :])
            here = xrow.at[zl_ * 2 + zh_, part]
            here[...] = val.astype(BF16)
            if m > 0:
                send(here, back.at[m - 1, part], r1_s.at[m - 1], r1_r.at[m - 1, dx], peer(m))
        return c

    lax.fori_loop(0, 4, x_back, 0)

    for m in (1, 2, 3):
        wait(pgl.at[m - 1], g1_r.at[m - 1])
    gs[zl] = pgs[zl] + pgl[2]
    gs[ozl] = pgl[0] + pgl[1]
    pltpu.make_async_copy(gs, gb.at[q], g2_r).start()

    def send_gate(i, c):
        send(gs, gb.at[q], g2_s, g2_r, dev(zl, (yc + i % 8) % 8, (x + i // 8) % 4, zh))
        return c

    lax.fori_loop(1, 32, send_gate, 0)

    def pair_back(i, c):
        dx = near_first(3 - i)
        xs = (x + dx) % 4
        part = chunk(xs)
        for m in (1, 2, 3):
            wait(back.at[m - 1, part], r1_r.at[m - 1, dx])
        xg[0, part, :] = (
            xrow[plane, part, :].astype(F32) + back[2, part, :].astype(F32)
        ).astype(BF16)
        xg[1, part, :] = (
            back[0, part, :].astype(F32) + back[1, part, :].astype(F32)
        ).astype(BF16)
        for s in (0, 1):
            zt = (zl + s) % 2
            spread(
                i, lambda r: xg.at[s, r], lambda r: ret.at[zt, r],
                r2_s.at[s], r2_r.at[s, dx], xs, dx,
            )
        return c

    lax.fori_loop(0, 4, pair_back, 0)

    for n in range(8):
        post[pl.ds(n * 128, 128), :] = posb[zl * 8 + n].T
    post[pl.ds(TOK, 128), :] = jnp.full((128, 8), -1.0, F32)
    pre[0:3, :, 0:SH] = jnp.zeros((3, CHUNK, SH), F32)

    def combine(i, c):
        dx = near_first(3 - i)
        xs = (x + 4 - dx) % 4
        for s in (0, 1):
            zt = (zl + s) % 2
            src = ret.at[zt, chunk(xs)]
            wait(src, r2_r.at[s, dx])

            def part_of(n, c):
                tile = post[chunk(n), :]
                place = (
                    lax.broadcasted_iota(jnp.int32, (CHUNK, CHUNK), 1) + (zt * 4 + xs) * CHUNK
                ).astype(F32)
                weigh = jnp.where(place == tile[:, 0:1], tile[:, 2:3], 0.0) + jnp.where(
                    place == tile[:, 1:2], tile[:, 3:4], 0.0
                )
                pre[n, :, 0:SH] += dot(weigh.astype(BF16), src[...])
                return c

            lax.fori_loop(0, 3, part_of, 0)
        return c

    lax.fori_loop(0, 4, combine, 0)
    for n, size in enumerate((CHUNK, CHUNK, TOK - 2 * CHUNK)):
        out[pl.ds(n * CHUNK, size), :] = pre[n, 0:size, 0:SH].astype(BF16)

    wait(gb, g2_r)
    keep = lax.broadcasted_iota(jnp.int32, (32, 8, 128), 1) == yc
    for s in (0, 1):
        vout[s] = jnp.sum(jnp.where(keep, gb[:, s], 0.0), axis=1)

    wait(posb.at[pl.ds(0, 15)], pos_s)
    for m in (0, 1, 2):
        wait(dyz.at[m], z_s.at[m])
        wait(back.at[m], r1_s.at[m])
        wait(pgl.at[m], g1_s.at[m])
    for m in (2, 3):
        wait(yg.at[0, pl.ds(0, ROWS - BLK)], b2_s.at[m])
    for s in (0, 1):
        wait(xg.at[s, pl.ds(0, ROWS - BLK)], r2_s.at[s])
    wait(gb.at[pl.ds(0, 31)], g2_s)


def expert_layer(pack, tokens, grad_out, gate_w, up_w, down_w):
    vmem = pl.BlockSpec(memory_space=pltpu.VMEM)
    hbm = pl.BlockSpec(memory_space=pl.ANY)
    dma = pltpu.SemaphoreType.DMA
    return pl.pallas_call(
        kernel,
        name="expert_layer",
        out_shape=(
            jax.ShapeDtypeStruct((TOK, SH), BF16),
            jax.ShapeDtypeStruct((2, 32, 128), F32),
        ),
        in_specs=[vmem, vmem, vmem, hbm, hbm, hbm],
        out_specs=(vmem, vmem),
        scratch_shapes=[
            pltpu.VMEM((WIDTH, HID), BF16),
            pltpu.VMEM((WIDTH, HID), BF16),
            pltpu.VMEM((HID, WIDTH), BF16),
            pltpu.VMEM((4, ROWS, SH), BF16),
            pltpu.VMEM((4, ROWS, SH), BF16),
            pltpu.VMEM((ROWS, SH), BF16),
            pltpu.VMEM((2, ROWS, SH), BF16),
            pltpu.VMEM((3, TOK, SH), BF16),
            pltpu.VMEM((2, ROWS, SH), BF16),
            pltpu.VMEM((3, ROWS, SH), BF16),
            pltpu.VMEM((2, ROWS, SH), BF16),
            pltpu.VMEM((4, CHUNK, HID), F32),
            pltpu.VMEM((2, CHUNK, HID), F32),
            pltpu.VMEM((16, 8, 128), F32),
            pltpu.VMEM((3 * CHUNK, 8), F32),
            pltpu.VMEM((2, 8, 128), F32),
            pltpu.VMEM((3, 8, 128), F32),
            pltpu.VMEM((2, 8, 128), F32),
            pltpu.VMEM((32, 2, 8, 128), F32),
            dma((3,)),
            dma, dma,
            dma((3,)), dma((3,)),
            dma((2,)), dma((4,)), dma((4,)),
            dma((3,)), dma((3, 4)),
            dma((4,)), dma((4, 4)),
            dma((3,)), dma((3, 4)),
            dma((2,)), dma((2, 4)),
            dma((3,)), dma((3,)),
            dma, dma,
        ],
        compiler_params=pltpu.CompilerParams(
            collective_id=0, has_side_effects=True, vmem_limit_bytes=64 << 20
        ),
        cost_estimate=pl.CostEstimate(
            flops=36_000_000_000, bytes_accessed=25_000_000, transcendentals=600_000
        ),
    )(pack, tokens, grad_out, gate_w, up_w, down_w)


def body(tokens, grad_out, expert_ids, gates, w_gate, w_up, w_down):
    tok_rows, topk = expert_ids.shape
    experts = 64
    onehot = (expert_ids[:, :, None] == jnp.arange(experts, dtype=jnp.int32)).astype(F32)
    member = jnp.sum(onehot, axis=1)
    lower = (jnp.arange(tok_rows)[:, None] > jnp.arange(tok_rows)[None, :]).astype(F32)
    earlier = jnp.dot(lower, member)
    slot = jnp.sum(earlier[:, None, :] * onehot, axis=2).astype(jnp.int32)
    slot = slot + lax.axis_index("tp") * CAP
    half, yc, x = expert_ids // 32, expert_ids % 32 // 4, expert_ids % 4
    code = (half * 4 + x) * CHUNK + yc * BLK + slot
    pack = jnp.concatenate(
        [code.astype(F32).T, gates.T, jnp.zeros((4, tok_rows), F32)], axis=0
    )
    grad_tokens, terms = expert_layer(
        pack, tokens, grad_out, w_gate[0], w_up[0], w_down[0]
    )
    grad_gates = terms.reshape(-1)[(half * 32 + x * 8 + yc) * 128 + slot]
    return (grad_tokens, grad_gates)


def solution(mesh):
    placed = (
        P("ctx", "tp"),
        P("ctx", "tp"),
        P(("ctx", "tp"), None),
        P(("ctx", "tp"), None),
        P(("ctx", "tp"), None, None),
        P(("ctx", "tp"), None, None),
        P(("ctx", "tp"), None, None),
    )
    return jax.shard_map(
        body,
        mesh=mesh,
        in_specs=placed,
        out_specs=(P("ctx", "tp"), P(("ctx", "tp"), None)),
        check_vma=False,
    )
```

profile of v0, /device:TPU:1, one launch (start us, length us, event | category | flops | bytes accessed | tf_op | source)
XLA Modules:
  0.0 225.4 jit_solution(10726335158386479660)
XLA Ops:
  0.6 0.7 convert_reduce_fusion
  1.3 0.1 fusion
  1.5 0.7 select_reduce_fusion
  2.2 1.3 compare_select_fusion
  3.4 0.7 convert_bitcast_fusion
  4.2 0.1 pad.2.clone
  4.2 1.3 maximum_maximum_fusion.pack
  5.6 215.4 %expert_layer.1 = (bf16[1024,512]{1,0:T(8,128)(2,1)}, f32[2,32,128]{2,1,0:T(8,128)}) custom-call(f32[8,128]{1,0:T(8,128)} %maximum_maximum_fusion.pack, bf16[1024,512]{1,0:T(8,128)(2,1)} %tok.1, bf16[1024,512]{1,0:T(8,128)(2,1)} %dy.1, bf16[4096,768]{1,0:T(8,128)(2,1)} %bitcast.10, bf16[4096,768]{1,0:T(8,128)(2,1)} %bitcast.11, bf16[768,4096]{1,0:T(8,128)(2,1)} %bitcast.12), custom_call_target="tpu_custom_call" | custom-call | flops 35999997952 | bytes 25000000 | tf_op jit(solution)/shard_map/expert_layer/pallas_call | solution.py:352
  221.0 0.0 copy-start
  221.0 0.8 copy.15
  221.8 0.1 reshape.12
  221.9 0.0 copy-done
  221.9 0.0 copy-start.1
  221.9 1.7 gather_fusion
  223.7 0.1 reshape.11
  223.8 0.6 copy.16
  224.5 0.0 copy-done.1
  224.5 1.0 copy.18
  (2 shorter events, 0.0 us)
Async XLA Ops:
  221.0 1.0 copy-start
  221.9 2.5 %copy-start.1 = (bf16[1024,512]{1,0:T(8,128)(2,1)S(1)}, bf16[1024,512]{1,0:T(8,128)(2,1)}, u32[]{:S(2)}) copy-start(bf16[1024,512]{1,0:T(8,128)(2,1)} %get-tuple-element.14) | copy-start | bytes 3145732
where the time goes:
time: 227 us; the launch traced here: 225 us
  Pallas kernels  215 us (95%)
  other arithmetic  4.72 us (2%)
  local copies, waits for them, and re-layouts  4.48 us (2%)
    pallas_call x1, Pallas kernels, expert_layer(): pl.pallas_call(kernel, name='expert_layer', out_shape=(jax.ShapeDtypeStru...  215 us

commit v1 on v0

v1 whole, which is shorter than its diff:
```python
import functools

import jax
import jax.numpy as jnp
from jax import lax
from jax.experimental import pallas as pl
from jax.experimental.pallas import tpu as pltpu
from jax.sharding import PartitionSpec as P

MESH = pl.DeviceIdType.MESH
FAR_FIRST = (
    (2, 2), (1, 2), (2, 1), (3, 2), (2, 3), (1, 1), (3, 3), (1, 3),
    (3, 1), (2, 0), (0, 2), (1, 0), (0, 1), (3, 0), (0, 3), (0, 0),
)
F32 = jnp.float32
BF16 = jnp.bfloat16

CAP = 6
BLK = 48
CHUNK = 384
ROWS = 1536
TOK = 1024
SH = 512
HID = 768
WIDTH = 4096
PART = 256


def dot(left, right):
    return jnp.dot(left, right, preferred_element_type=F32)


def dot_last(left, right):
    return lax.dot_general(left, right, (((1,), (1,)), ((), ())), preferred_element_type=F32)


def kernel(
    routes, tok, dy, wg_hbm, wu_hbm, wd_hbm,
    out, gate_out,
    wg, wu, wd, xrow, yrow, stage, buf, dyz, back, ret,
    pre, dab, pack, posb, post, pgs, pgl, gs, gb,
    w_sem, pos_s, pos_r, z_s, z_r, a1x_r, a1p_r, a2_s, a2_r,
    b_s, b2_r, r1_s, r1_r, r2_s, r2_r, p3_s, p3_r, g1_s, g1_r, g2_s, g2_r,
):
    ctx, tp = lax.axis_index("ctx"), lax.axis_index("tp")
    zl, yc, x, zh = ctx // 8, ctx % 8, tp // 2, tp % 2
    ozl = 1 - zl
    plane = zl * 2 + zh
    q = x * 8 + yc

    def dev(zl_, yc_, x_, zh_):
        return (zl_ * 8 + yc_, x_ * 2 + zh_)

    def plane_of(m):
        return (zl + ((m + 1) // 2) % 2) % 2, (zh + m // 2) % 2

    def place_of(m):
        zl_, zh_ = plane_of(m)
        return zl_ * 2 + zh_

    def peer(m):
        zl_, zh_ = plane_of(m)
        return dev(zl_, yc, x, zh_)

    def near_first(i):
        return i + (i // 2) * (5 - 2 * i)

    def rows(n):
        return pl.ds(pl.multiple_of(n * BLK, BLK), BLK)

    def chunk(n):
        return pl.ds(pl.multiple_of(n * CHUNK, CHUNK), CHUNK)

    def shard(n):
        return pl.ds(pl.multiple_of(n * SH, SH), SH)

    def send(src, dst, s_sem, r_sem, to):
        pltpu.make_async_remote_copy(
            src_ref=src, dst_ref=dst, send_sem=s_sem, recv_sem=r_sem,
            device_id=to, device_id_type=MESH,
        ).start()

    def wait(ref, sem):
        pltpu.make_async_copy(ref, ref, sem).wait()

    bar = pltpu.get_barrier_semaphore()

    def greet_plane(i, c):
        to = dev(zl, (yc + i % 8) % 8, (x + i // 8) % 4, zh)
        pl.semaphore_signal(bar, inc=1, device_id=to, device_id_type=MESH)
        return c

    def greet_other(i, c):
        zl_, zh_ = plane_of(1 + i // 4)
        to = dev(zl_, yc, (x + i % 4) % 4, zh_)
        pl.semaphore_signal(bar, inc=1, device_id=to, device_id_type=MESH)
        return c

    lax.fori_loop(0, 12, greet_other, 0)
    lax.fori_loop(1, 32, greet_plane, 0)
    loads = [
        pltpu.make_async_copy(wg_hbm, wg, w_sem.at[0]),
        pltpu.make_async_copy(wu_hbm, wu, w_sem.at[1]),
        pltpu.make_async_copy(wd_hbm, wd, w_sem.at[2]),
    ]
    for load in loads:
        load.start()

    ids = [routes[k : k + 1, :] for k in (0, 1)]
    expert = lax.broadcasted_iota(jnp.int32, (64, 128), 0).astype(F32)
    named = [jnp.where(expert == e, 1.0, 0.0) for e in ids]
    before = lax.broadcasted_iota(jnp.int32, (128, 128), 0) < lax.broadcasted_iota(
        jnp.int32, (128, 128), 1
    )
    earlier = dot((named[0] + named[1]).astype(BF16), jnp.where(before, 1.0, 0.0).astype(BF16))
    first = (tp * CAP).astype(F32)
    for k in (0, 1):
        slot = jnp.sum(named[k] * earlier, axis=0, keepdims=True) + first
        half = jnp.floor(ids[k] * (1 / 32))
        rest = ids[k] - half * 32.0
        line = jnp.floor(rest * 0.25)
        column = rest - line * 4.0
        pack[k : k + 1, :] = (half * 4.0 + column) * CHUNK + line * BLK + slot
        pack[2 + k : 3 + k, :] = routes[2 + k : 3 + k, :]
        pack[4 + k : 5 + k, :] = half * 32.0 + column * 8.0 + line
        pack[6 + k : 7 + k, :] = slot

    pl.semaphore_wait(bar, 43)

    top, low = pl.ds(0, TOK // 2), pl.ds(TOK // 2, TOK // 2)
    send(dy.at[top], dyz.at[0, top], z_s.at[0], z_r.at[0, 0], peer(1))
    send(dy.at[low], dyz.at[1, low], z_s.at[1], z_r.at[1, 1], peer(2))
    mine = posb.at[zl * 8 + tp]
    pltpu.make_async_copy(pack, mine, pos_r).start()

    def send_pos(i, c):
        to = dev((zl + i // 8) % 2, yc, (x + (i // 2) % 4) % 4, (zh + i % 2) % 2)
        send(pack, mine, pos_s, pos_r, to)
        return c

    lax.fori_loop(1, 16, send_pos, 0)
    wait(posb, pos_r)

    def select(zl_, c):
        place = (lax.broadcasted_iota(jnp.int32, (CHUNK, 128), 0) + c * CHUNK).astype(F32)
        parts = []
        for n in range(8):
            tile = posb[zl_ * 8 + n]
            hit = (place == tile[0:1]) | (place == tile[1:2])
            parts.append(jnp.where(hit, 1.0, 0.0).astype(BF16))
        return jnp.concatenate(parts, axis=1)

    def spread(src_of, dst, s_sem, r_sem_of):
        def side(n, c):
            dc = 1 - n
            for dx, dy in FAR_FIRST:
                xd, ycd = (x + dx) % 4, (yc // 2 + dy) % 4 * 2 + (yc + dc) % 2
                src = src_of(xd * 8 + ycd)
                go = functools.partial(
                    send, src, dst, s_sem, r_sem_of(dx), dev(zl, ycd, xd, zh)
                )
                if dx + dy > 0:
                    go()
                    continue

                @pl.when(dc == 0)
                def _():
                    pltpu.make_async_copy(src, dst, s_sem).start()

                pl.when(dc > 0)(go)
            return c

        lax.fori_loop(0, 2, side, 0)

    def arrived(ref, xs, sem, dx):
        @pl.when(dx > 0)
        def _():
            wait(ref.at[chunk(xs)], sem)

        @pl.when(dx == 0)
        def _():
            wait(ref.at[pl.ds(0, CHUNK - BLK)], sem)

    def left(b):
        wait(buf.at[pl.ds(0, ROWS)], b_s.at[b])

    def batch(b, slot, src, zl_src, zl_dst, dst, r_sem_of):
        def step(xd, c):
            picked = dot(select(zl_src, zl_dst * 4 + xd), src[...])
            buf[chunk(4 * slot + xd), :] = picked.astype(BF16)
            return c

        lax.fori_loop(0, 4, step, 0)
        spread(lambda k: buf.at[rows(32 * slot + k)], dst, b_s.at[b], r_sem_of)

    def x_out(b, slot, s):
        dst = stage.at[rows(q)] if s else xrow.at[plane, rows(q)]
        sem = a1p_r if s else a1x_r
        batch(b, slot, tok, zl, (zl + s) % 2, dst, lambda dx: sem.at[dx])

    def y_out(b, slot, m):
        src = dy if m == 0 else dyz.at[m - 1]
        dst = yrow.at[place_of(m), rows(q)]
        batch(b, slot, src, plane_of(m)[0], zl, dst, lambda dx: b2_r.at[m, dx])

    def forward_near(dx):
        xs = (x + 4 - dx) % 4
        part = chunk(xs)
        arrived(stage, xs, a1p_r.at[dx], dx)
        for m in (1, 2):
            send(stage.at[part], xrow.at[plane, part], a2_s.at[m - 1], a2_r.at[m - 1, dx], peer(m))

    def forward_far(dx):
        part = chunk((x + 4 - dx) % 4)
        send(xrow.at[plane, part], xrow.at[plane, part], a2_s.at[2], a2_r.at[2, dx], peer(3))

    def base_of(m):
        return 0 if m in (1, 2) else 3

    def take_x(m, dx):
        xs = (x + 4 - dx) % 4
        src = xrow.at[place_of(m), chunk(xs)]
        if m > 0:
            wait(src, a2_r.at[m - 1, dx])
        part = shard(xs * 2 + plane_of(m)[1])
        pre[base_of(m)] += dot(src[...], wg[part, :])
        pre[base_of(m) + 1] += dot(src[...], wu[part, :])

    def take_y(m, dx):
        xs = (x + 4 - dx) % 4
        arrived(yrow.at[place_of(m)], xs, b2_r.at[m, dx], dx)
        part = shard(xs * 2 + plane_of(m)[1])
        pre[base_of(m) + 2] += dot_last(yrow[place_of(m), chunk(xs), :], wd[:, part])

    def each(f):
        def step(i, c):
            f(near_first(i))
            return c

        lax.fori_loop(0, 4, step, 0)

    x_out(0, 0, 1)
    send(dy.at[low], dyz.at[0, low], z_s.at[0], z_r.at[0, 1], peer(1))
    send(dy.at[top], dyz.at[1, top], z_s.at[1], z_r.at[1, 0], peer(2))
    x_out(1, 1, 0)
    wait(dyz.at[0, top], z_r.at[0, 0])
    send(dyz.at[0, top], dyz.at[2, top], z_s.at[2], z_r.at[2, 0], peer(2))
    wait(dyz.at[1, low], z_r.at[1, 1])
    send(dyz.at[1, low], dyz.at[2, low], z_s.at[2], z_r.at[2, 1], peer(1))
    wait(dyz.at[0, low], z_r.at[0, 1])
    y_out(2, 2, 1)
    left(0)
    for dx in (0, 1, 3, 2):
        forward_near(dx)
    wait(dyz.at[1, top], z_r.at[1, 0])
    y_out(3, 0, 2)
    pre[...] = jnp.zeros_like(pre)
    for load in loads:
        load.wait()
    left(1)
    for dx in (0, 1, 3, 2):
        arrived(xrow.at[plane], (x + 4 - dx) % 4, a1x_r.at[dx], dx)
    each(lambda dx: take_x(0, dx))
    left(2)
    y_out(4, 2, 0)
    each(lambda dx: (take_x(1, dx), take_x(2, dx)))
    for m in (0, 1):
        wait(xrow.at[0], a2_s.at[m])
    for dx in (0, 1, 3, 2):
        forward_far(dx)
    wait(dyz.at[2, top], z_r.at[2, 0])
    wait(dyz.at[2, low], z_r.at[2, 1])
    left(3)
    y_out(5, 0, 3)
    each(lambda dx: take_y(1, dx))
    each(lambda dx: take_y(2, dx))

    def inner(g, dst):
        base = 0 if g else 3

        def step(n, c):
            part = rows(n)
            av, bv, hv = pre[base, part, :], pre[base + 1, part, :], pre[base + 2, part, :]
            sigma = 1.0 / (1.0 + jnp.exp(-av))
            active = av * sigma
            hidden = (active * bv).astype(BF16).astype(F32)
            dst[part, 0:HID] = (hv * bv * sigma * (1.0 + av * (1.0 - sigma))).astype(BF16)
            dst[part, HID : 2 * HID] = (hv * active).astype(BF16)
            gate = jnp.sum(hidden * hv, axis=1, keepdims=True)
            diag = lax.broadcasted_iota(jnp.int32, (BLK, 128), 0) == lax.broadcasted_iota(
                jnp.int32, (BLK, 128), 1
            )
            pgs[g, pl.ds(n, 1), :] = jnp.sum(jnp.where(diag, gate, 0.0), axis=0, keepdims=True)
            return c

        lax.fori_loop(0, 8, step, 0)

    def grad_x(src, m, xs):
        piece = shard(xs * 2 + plane_of(m)[1])
        val = dot_last(src[0:CHUNK, 0:HID], wg[piece, :])
        val += dot_last(src[0:CHUNK, HID : 2 * HID], wu[piece, :])
        here = xrow.at[place_of(m), chunk(xs)]
        here[...] = val.astype(BF16)
        return here

    inner(1, dab)
    for m in (1, 2):
        send(pgs.at[1], pgl.at[m - 1], g1_s.at[m - 1], g1_r.at[m - 1], peer(m))

    def back_near(dx):
        for m in (1, 2):
            grad_x(dab, m, (x + dx) % 4)

    each(back_near)
    left(4)
    each(lambda dx: take_y(0, dx))

    for n in range(8):
        post[pl.ds(n * 128, 128), :] = posb[zl * 8 + n].T

    def tokens_of(n):
        return pl.ds(pl.multiple_of(n * PART, PART), PART)

    def weigh(n, first, size):
        tile = post[tokens_of(n), :]
        place = (lax.broadcasted_iota(jnp.int32, (PART, size), 1) + first).astype(F32)
        hit = jnp.where(place == tile[:, 0:1], tile[:, 2:3], 0.0)
        return (hit + jnp.where(place == tile[:, 1:2], tile[:, 3:4], 0.0)).astype(BF16)

    wait(dyz.at[2], z_s.at[2])

    def weigh_own(n, c):
        for p in range(3):
            dyz[p, tokens_of(n), :] = weigh(n, zl * ROWS + p * SH, SH)
        return c

    lax.fori_loop(0, 4, weigh_own, 0)

    def total_own(n, k):
        total = dot(dyz[0, tokens_of(n), :], ret[k, 0:SH, :])
        for p in (1, 2):
            total += dot(dyz[p, tokens_of(n), :], ret[k, p * SH : (p + 1) * SH, :])
        return total

    wait(xrow.at[plane], a2_s.at[2])
    for i in (2, 3, 1, 0):
        part = chunk((x + i) % 4)
        for m in (1, 2):
            send(
                xrow.at[place_of(m), part], back.at[m - 1, part],
                r1_s.at[m - 1], r1_r.at[m - 1, i], peer(m),
            )

    each(lambda dx: take_x(3, dx))
    left(5)
    each(lambda dx: take_y(3, dx))
    inner(0, wd)
    send(pgs.at[0], pgl.at[2], g1_s.at[2], g1_r.at[2], peer(3))

    def back_own(m, k):
        each(lambda dx: grad_x(wd, m, dx))
        spread(
            lambda n: xrow.at[place_of(m), rows(n)], ret.at[k, rows(q)],
            r2_s.at[k], lambda dx: r2_r.at[k, dx],
        )

    back_own(3, 2)

    def pair_back():
        def step(dx):
            part = chunk((x + dx) % 4)
            for m in (1, 2):
                wait(back.at[m - 1, part], r1_r.at[m - 1, dx])
            pair = back[0, part, :].astype(F32) + back[1, part, :].astype(F32)
            buf[part, :] = pair.astype(BF16)

        each(step)
        spread(
            lambda n: buf.at[rows(n)], ret.at[0, rows(q)], r2_s.at[0],
            lambda dx: r2_r.at[0, dx],
        )

    wait(xrow.at[0], r2_s.at[2])
    back_own(0, 1)

    for dx in range(4):
        arrived(ret.at[2], (x + 4 - dx) % 4, r2_r.at[2, dx], dx)

    def far_total(n, c):
        here = pl.ds(pl.multiple_of(ROWS + n * PART, PART), PART)
        buf[here, :] = total_own(n, 2).astype(BF16)
        send(buf.at[here], out.at[tokens_of(n)], p3_s.at[n], p3_r.at[n], peer(3))
        return c

    lax.fori_loop(0, 4, far_total, 0)
    pair_back()

    for m in (1, 2, 3):
        wait(pgl.at[m - 1], g1_r.at[m - 1])
    gs[zl] = pgs[0] + pgl[2]
    gs[ozl] = pgl[0] + pgl[1]
    pltpu.make_async_copy(gs, gb.at[q], g2_r).start()

    def send_gate(i, c):
        send(gs, gb.at[q], g2_s, g2_r, dev(zl, (yc + i % 8) % 8, (x + i // 8) % 4, zh))
        return c

    lax.fori_loop(1, 32, send_gate, 0)

    wait(xrow.at[0], r2_s.at[1])
    for dx in range(4):
        arrived(ret.at[1], (x + 4 - dx) % 4, r2_r.at[1, dx], dx)

    def own_total(n, c):
        pre[n, 0:PART, 0:SH] = total_own(n, 1)
        return c

    lax.fori_loop(0, 4, own_total, 0)

    wait(gb, g2_r)
    keep = lax.broadcasted_iota(jnp.int32, (32, 8, 128), 1) == yc
    terms = jnp.concatenate([jnp.sum(jnp.where(keep, gb[:, s], 0.0), axis=1) for s in (0, 1)])
    terms = terms.T
    coarse = terms.astype(BF16)
    fine = (terms - coarse.astype(F32)).astype(BF16)
    lane = lax.broadcasted_iota(jnp.int32, (128, 128), 0).astype(F32)
    for k in (0, 1):
        at = jnp.where(expert == pack[4 + k : 5 + k, :], 1.0, 0.0).astype(BF16)
        found = dot(coarse, at) + dot(fine, at)
        gate_out[k : k + 1, :] = jnp.sum(
            jnp.where(lane == pack[6 + k : 7 + k, :], found, 0.0), axis=0, keepdims=True
        )

    wait(xrow.at[0], r2_s.at[0])

    def pair_total(dx):
        xs = (x + 4 - dx) % 4
        arrived(ret.at[0], xs, r2_r.at[0, dx], dx)

        def part_of(n, c):
            weights = weigh(n, (ozl * 4 + xs) * CHUNK, CHUNK)
            pre[n, 0:PART, 0:SH] += dot(weights, ret[0, chunk(xs), :])
            return c

        lax.fori_loop(0, 4, part_of, 0)

    lax.fori_loop(0, 4, lambda i, c: (pair_total(near_first(3 - i)), c)[1], 0)

    def finish(n, c):
        here = tokens_of(n)
        wait(out.at[here], p3_r.at[n])
        out[here, :] = (pre[n, 0:PART, 0:SH] + out[here, :].astype(F32)).astype(BF16)
        wait(out.at[here], p3_s.at[n])
        return c

    lax.fori_loop(0, 4, finish, 0)

    wait(posb.at[pl.ds(0, 15)], pos_s)
    for m in (0, 1, 2):
        wait(pgl.at[m], g1_s.at[m])
    for m in (0, 1):
        wait(dyz.at[m], z_s.at[m])
        wait(back.at[m], r1_s.at[m])
    wait(gb.at[pl.ds(0, 31)], g2_s)


def expert_layer(routes, tokens, grad_out, gate_w, up_w, down_w):
    vmem = pl.BlockSpec(memory_space=pltpu.VMEM)
    hbm = pl.BlockSpec(memory_space=pl.ANY)
    dma = pltpu.SemaphoreType.DMA
    return pl.pallas_call(
        kernel,
        name="expert_layer",
        out_shape=(
            jax.ShapeDtypeStruct((TOK, SH), BF16),
            jax.ShapeDtypeStruct((2, 128), F32),
        ),
        in_specs=[vmem, vmem, vmem, hbm, hbm, hbm],
        out_specs=(vmem, vmem),
        scratch_shapes=[
            pltpu.VMEM((WIDTH, HID), BF16),
            pltpu.VMEM((WIDTH, HID), BF16),
            pltpu.VMEM((HID, WIDTH), BF16),
            pltpu.VMEM((4, ROWS, SH), BF16),
            pltpu.VMEM((4, ROWS, SH), BF16),
            pltpu.VMEM((ROWS, SH), BF16),
            pltpu.VMEM((3 * ROWS, SH), BF16),
            pltpu.VMEM((3, TOK, SH), BF16),
            pltpu.VMEM((2, ROWS, SH), BF16),
            pltpu.VMEM((3, ROWS, SH), BF16),
            pltpu.VMEM((6, CHUNK, HID), F32),
            pltpu.VMEM((CHUNK, 2 * HID), BF16),
            pltpu.VMEM((8, 128), F32),
            pltpu.VMEM((16, 8, 128), F32),
            pltpu.VMEM((TOK, 8), F32),
            pltpu.VMEM((2, 8, 128), F32),
            pltpu.VMEM((3, 8, 128), F32),
            pltpu.VMEM((2, 8, 128), F32),
            pltpu.VMEM((32, 2, 8, 128), F32),
            dma((3,)),
            dma, dma,
            dma((3,)), dma((3, 2)),
            dma((4,)), dma((4,)),
            dma((3,)), dma((3, 4)),
            dma((6,)), dma((4, 4)),
            dma((2,)), dma((2, 4)),
            dma((3,)), dma((3, 4)),
            dma((4,)), dma((4,)),
            dma((3,)), dma((3,)),
            dma, dma,
        ],
        compiler_params=pltpu.CompilerParams(
            collective_id=0, has_side_effects=True, vmem_limit_bytes=64 << 20
        ),
        cost_estimate=pl.CostEstimate(
            flops=36_000_000_000, bytes_accessed=25_000_000, transcendentals=600_000
        ),
    )(routes, tokens, grad_out, gate_w, up_w, down_w)


def body(tokens, grad_out, expert_ids, gates, w_gate, w_up, w_down):
    tok_rows, topk = expert_ids.shape
    routes = jnp.concatenate([expert_ids.astype(F32), gates], axis=1).T
    grad_tokens, grad_gates = expert_layer(
        routes, tokens, grad_out, w_gate[0], w_up[0], w_down[0]
    )
    return (grad_tokens, grad_gates.T)


def solution(mesh):
    placed = (
        P("ctx", "tp"),
        P("ctx", "tp"),
        P(("ctx", "tp"), None),
        P(("ctx", "tp"), None),
        P(("ctx", "tp"), None, None),
        P(("ctx", "tp"), None, None),
        P(("ctx", "tp"), None, None),
    )
    return jax.shard_map(
        body,
        mesh=mesh,
        in_specs=placed,
        out_specs=(P("ctx", "tp"), P(("ctx", "tp"), None)),
        check_vma=False,
    )
```

time: 227 us -> 214 us (0.943)
  Pallas kernels: 215 us -> 207 us
  other arithmetic: 4.72 us -> 1.94 us
    pallas_call x1, Pallas kernels: 215 us -> 207 us  [expert_layer(): pl.pallas_call(kernel, name='expert_layer', out_shape=(jax.ShapeDtypeStru...]
where the time goes in v1:
time: 214 us
  Pallas kernels  207 us (97%)
  local copies, waits for them, and re-layouts  3.5 us (2%)
    pallas_call x1, Pallas kernels, expert_layer(): pl.pallas_call(kernel, name='expert_layer', out_shape=(jax.ShapeDtypeStru...  207 us

profile of v1, /device:TPU:1, one launch (start us, length us, event | category | flops | bytes accessed | tf_op | source)
XLA Modules:
  0.0 213.6 jit_solution(16118755645566705168)
XLA Ops:
  0.6 0.7 convert_element_type.3
  1.3 1.3 maximum_bitcast_fusion.routes
  2.6 207.5 %expert_layer.1 = (bf16[1024,512]{1,0:T(8,128)(2,1)}, f32[2,128]{1,0:T(2,128)}) custom-call(f32[4,128]{1,0:T(4,128)} %maximum_bitcast_fusion.routes, bf16[1024,512]{1,0:T(8,128)(2,1)} %tok.1, bf16[1024,512]{1,0:T(8,128)(2,1)} %dy.1, bf16[4096,768]{1,0:T(8,128)(2,1)} %bitcast.7, bf16[4096,768]{1,0:T(8,128)(2,1)} %bitcast.8, bf16[768,4096]{1,0:T(8,128)(2,1)} %bitcast.9), custom_call_target="tpu_custom_call" | custom-call | flops 35999997952 | bytes 25000000 | tf_op jit(solution)/shard_map/expert_layer/pallas_call | solution.py:471
  210.1 2.3 %copy.11 = bf16[1024,512]{1,0:T(8,128)(2,1)} copy(bf16[1024,512]{1,0:T(8,128)(2,1)} %get-tuple-element.8) | data formatting | bytes 2097152
  212.3 1.2 copy.12

commit v2 on v1

--- a/solution.py
+++ b/solution.py
@@ -35,7 +35,7 @@
 
 
 def kernel(
-    routes, tok, dy, wg_hbm, wu_hbm, wd_hbm,
+    names, gates, tok, dy, wg_hbm, wu_hbm, wd_hbm,
     out, gate_out,
     wg, wu, wd, xrow, yrow, stage, buf, dyz, back, ret,
     pre, dab, pack, posb, post, pgs, pgl, gs, gb,
@@ -106,7 +106,7 @@
     for load in loads:
         load.start()
 
-    ids = [routes[k : k + 1, :] for k in (0, 1)]
+    ids = [names[k : k + 1, :].astype(F32) for k in (0, 1)]
     expert = lax.broadcasted_iota(jnp.int32, (64, 128), 0).astype(F32)
     named = [jnp.where(expert == e, 1.0, 0.0) for e in ids]
     before = lax.broadcasted_iota(jnp.int32, (128, 128), 0) < lax.broadcasted_iota(
@@ -121,7 +121,7 @@
         line = jnp.floor(rest * 0.25)
         column = rest - line * 4.0
         pack[k : k + 1, :] = (half * 4.0 + column) * CHUNK + line * BLK + slot
-        pack[2 + k : 3 + k, :] = routes[2 + k : 3 + k, :]
+        pack[2 + k : 3 + k, :] = gates[k : k + 1, :]
         pack[4 + k : 5 + k, :] = half * 32.0 + column * 8.0 + line
         pack[6 + k : 7 + k, :] = slot
 
@@ -172,6 +172,26 @@
 
         lax.fori_loop(0, 2, side, 0)
 
+    def spread_at(dx, src_of, dst, s_sem, r_sem):
+        xd = (x + dx) % 4
+
+        def one(j, c):
+            ycd = (yc + j) % 8
+            src = src_of(xd * 8 + ycd)
+            own = dx * 8 + j == 0
+
+            @pl.when(own)
+            def _():
+                pltpu.make_async_copy(src, dst, s_sem).start()
+
+            @pl.when(jnp.logical_not(own))
+            def _():
+                send(src, dst, s_sem, r_sem, dev(zl, ycd, xd, zh))
+
+            return c
+
+        lax.fori_loop(0, 8, one, 0)
+
     def arrived(ref, xs, sem, dx):
         @pl.when(dx > 0)
         def _():
@@ -185,13 +205,21 @@
         wait(buf.at[pl.ds(0, ROWS)], b_s.at[b])
 
     def batch(b, slot, src, zl_src, zl_dst, dst, r_sem_of):
-        def step(xd, c):
+        def step(i, c):
+            dx = near_first(3 - i)
+            xd = (x + dx) % 4
             picked = dot(select(zl_src, zl_dst * 4 + xd), src[...])
             buf[chunk(4 * slot + xd), :] = picked.astype(BF16)
+            if b < 0:
+                spread_at(dx, src_of, dst, b_s.at[b], r_sem_of(dx))
             return c
 
+        def src_of(k):
+            return buf.at[rows(32 * slot + k)]
+
         lax.fori_loop(0, 4, step, 0)
-        spread(lambda k: buf.at[rows(32 * slot + k)], dst, b_s.at[b], r_sem_of)
+        if b >= 0:
+            spread(src_of, dst, b_s.at[b], r_sem_of)
 
     def x_out(b, slot, s):
         dst = stage.at[rows(q)] if s else xrow.at[plane, rows(q)]
@@ -336,6 +364,41 @@
 
     lax.fori_loop(0, 4, weigh_own, 0)
 
+    def near_place(n, p):
+        if p == 2:
+            base = TOK + n % 2 * PART
+            late = pl.ds(pl.multiple_of(base, PART), PART)
+            return late, pl.ds(pl.multiple_of(2 * ROWS + base, PART), PART)
+        base = n * PART
+        if p == 1:
+            return pl.ds(pl.multiple_of(base, PART), PART), None
+        return None, pl.ds(pl.multiple_of(2 * ROWS + base, PART), PART)
+
+    def weigh_near(n, c):
+        first = ozl * ROWS
+        buf[near_place(n, 0)[1], :] = weigh(n, first, SH)
+        stage[near_place(n, 1)[0], :] = weigh(n, first + SH, SH)
+        in_stage, in_buf = near_place(n, 2)
+        tile = weigh(n, first + 2 * SH, SH)
+
+        @pl.when(n < 2)
+        def _():
+            stage[in_stage, :] = tile
+
+        @pl.when(n >= 2)
+        def _():
+            buf[in_buf, :] = tile
+
+        return c
+
+    def total_near(n):
+        total = dot(buf[near_place(n, 0)[1], :], ret[0, 0:SH, :])
+        total += dot(stage[near_place(n, 1)[0], :], ret[0, SH : 2 * SH, :])
+        in_stage, in_buf = near_place(n, 2)
+        last = jnp.where(n < 2, stage[in_stage, :], buf[in_buf, :])
+        return total + dot(last, ret[0, 2 * SH : 3 * SH, :])
+
+
     def total_own(n, k):
         total = dot(dyz[0, tokens_of(n), :], ret[k, 0:SH, :])
         for p in (1, 2):
@@ -351,20 +414,31 @@
                 r1_s.at[m - 1], r1_r.at[m - 1, i], peer(m),
             )
 
+    lax.fori_loop(0, 4, weigh_near, 0)
+
     each(lambda dx: take_x(3, dx))
     left(5)
     each(lambda dx: take_y(3, dx))
     inner(0, wd)
     send(pgs.at[0], pgl.at[2], g1_s.at[2], g1_r.at[2], peer(3))
 
-    def back_own(m, k):
-        each(lambda dx: grad_x(wd, m, dx))
-        spread(
-            lambda n: xrow.at[place_of(m), rows(n)], ret.at[k, rows(q)],
-            r2_s.at[k], lambda dx: r2_r.at[k, dx],
-        )
-
-    back_own(3, 2)
+    def back_own(m, k, at_once):
+        def src_of(n):
+            return xrow.at[place_of(m), rows(n)]
+
+        def step(i, c):
+            dx = near_first(3 - i)
+            grad_x(wd, m, (x + dx) % 4)
+            if at_once:
+                spread_at(dx, src_of, ret.at[k, rows(q)], r2_s.at[k], r2_r.at[k, dx])
+            return c
+
+        lax.fori_loop(0, 4, step, 0)
+        if not at_once:
+            spread(src_of, ret.at[k, rows(q)], r2_s.at[k], lambda dx: r2_r.at[k, dx])
+
+    back_own(3, 2, False)
+    back_own(0, 1, False)
 
     def pair_back():
         def step(dx):
@@ -381,8 +455,6 @@
         )
 
     wait(xrow.at[0], r2_s.at[2])
-    back_own(0, 1)
-
     for dx in range(4):
         arrived(ret.at[2], (x + 4 - dx) % 4, r2_r.at[2, dx], dx)
 
@@ -433,23 +505,14 @@
 
     wait(xrow.at[0], r2_s.at[0])
 
-    def pair_total(dx):
-        xs = (x + 4 - dx) % 4
-        arrived(ret.at[0], xs, r2_r.at[0, dx], dx)
-
-        def part_of(n, c):
-            weights = weigh(n, (ozl * 4 + xs) * CHUNK, CHUNK)
-            pre[n, 0:PART, 0:SH] += dot(weights, ret[0, chunk(xs), :])
-            return c
-
-        lax.fori_loop(0, 4, part_of, 0)
-
-    lax.fori_loop(0, 4, lambda i, c: (pair_total(near_first(3 - i)), c)[1], 0)
+    for dx in range(4):
+        arrived(ret.at[0], (x + 4 - dx) % 4, r2_r.at[0, dx], dx)
 
     def finish(n, c):
         here = tokens_of(n)
+        total = pre[n, 0:PART, 0:SH] + total_near(n)
         wait(out.at[here], p3_r.at[n])
-        out[here, :] = (pre[n, 0:PART, 0:SH] + out[here, :].astype(F32)).astype(BF16)
+        out[here, :] = (total + out[here, :].astype(F32)).astype(BF16)
         wait(out.at[here], p3_s.at[n])
         return c
 
@@ -464,7 +527,7 @@
     wait(gb.at[pl.ds(0, 31)], g2_s)
 
 
-def expert_layer(routes, tokens, grad_out, gate_w, up_w, down_w):
+def expert_layer(names, gates, tokens, grad_out, gate_w, up_w, down_w):
     vmem = pl.BlockSpec(memory_space=pltpu.VMEM)
     hbm = pl.BlockSpec(memory_space=pl.ANY)
     dma = pltpu.SemaphoreType.DMA
@@ -475,7 +538,7 @@
             jax.ShapeDtypeStruct((TOK, SH), BF16),
             jax.ShapeDtypeStruct((2, 128), F32),
         ),
-        in_specs=[vmem, vmem, vmem, hbm, hbm, hbm],
+        in_specs=[vmem, vmem, vmem, vmem, hbm, hbm, hbm],
         out_specs=(vmem, vmem),
         scratch_shapes=[
             pltpu.VMEM((WIDTH, HID), BF16),
@@ -515,14 +578,12 @@
         cost_estimate=pl.CostEstimate(
             flops=36_000_000_000, bytes_accessed=25_000_000, transcendentals=600_000
         ),
-    )(routes, tokens, grad_out, gate_w, up_w, down_w)
+    )(names, gates, tokens, grad_out, gate_w, up_w, down_w)
 
 
 def body(tokens, grad_out, expert_ids, gates, w_gate, w_up, w_down):
-    tok_rows, topk = expert_ids.shape
-    routes = jnp.concatenate([expert_ids.astype(F32), gates], axis=1).T
     grad_tokens, grad_gates = expert_layer(
-        routes, tokens, grad_out, w_gate[0], w_up[0], w_down[0]
+        expert_ids.T, gates.T, tokens, grad_out, w_gate[0], w_up[0], w_down[0]
     )
     return (grad_tokens, grad_gates.T)
 

time: 214 us -> 204 us (0.953)
  Pallas kernels: 207 us -> 199 us
    pallas_call x1, Pallas kernels: 207 us -> 199 us  [expert_layer(): pl.pallas_call(kernel, name='expert_layer', out_shape=(jax.ShapeDtypeStru...]
where the time goes in v2:
time: 204 us; the launch traced here: 203 us
  Pallas kernels  199 us (98%)
  local copies, waits for them, and re-layouts  3.5 us (2%)
    pallas_call x1, Pallas kernels, expert_layer(): pl.pallas_call(kernel, name='expert_layer', out_shape=(jax.ShapeDtypeStru...  199 us

profile of v2, /device:TPU:1, one launch (start us, length us, event | category | flops | bytes accessed | tf_op | source)
XLA Modules:
  0.0 202.8 jit_solution(6432775956157819403)
XLA Ops:
  0.6 198.7 %expert_layer.1 = (bf16[1024,512]{1,0:T(8,128)(2,1)}, f32[2,128]{1,0:T(2,128)}) custom-call(s32[2,128]{1,0:T(2,128)} %bitcast.10, f32[2,128]{1,0:T(2,128)} %bitcast.11, bf16[1024,512]{1,0:T(8,128)(2,1)} %tok.1, bf16[1024,512]{1,0:T(8,128)(2,1)} %dy.1, bf16[4096,768]{1,0:T(8,128)(2,1)} %bitcast.7, bf16[4096,768]{1,0:T(8,128)(2,1)} %bitcast.8, ...), custom_call_target="tpu_custom_call" | custom-call | flops 35999997952 | bytes 25000000 | tf_op jit(solution)/shard_map/expert_layer/pallas_call | solution.py:534
  199.3 2.3 %copy.11 = bf16[1024,512]{1,0:T(8,128)(2,1)} copy(bf16[1024,512]{1,0:T(8,128)(2,1)} %get-tuple-element.8) | data formatting | bytes 2097152
  201.6 1.2 copy.12

commit v3 on v2

--- a/solution.py
+++ b/solution.py
@@ -8,9 +8,9 @@
 from jax.sharding import PartitionSpec as P
 
 MESH = pl.DeviceIdType.MESH
-FAR_FIRST = (
-    (2, 2), (1, 2), (2, 1), (3, 2), (2, 3), (1, 1), (3, 3), (1, 3),
-    (3, 1), (2, 0), (0, 2), (1, 0), (0, 1), (3, 0), (0, 3), (0, 0),
+STEPS = (
+    (2, 2), (1, 0), (0, 1), (2, 1), (3, 0), (0, 3), (1, 2), (2, 3),
+    (3, 2), (1, 1), (3, 3), (2, 0), (0, 2), (1, 3), (3, 1), (0, 0),
 )
 F32 = jnp.float32
 BF16 = jnp.bfloat16
@@ -153,7 +153,7 @@
     def spread(src_of, dst, s_sem, r_sem_of):
         def side(n, c):
             dc = 1 - n
-            for dx, dy in FAR_FIRST:
+            for dx, dy in STEPS:
                 xd, ycd = (x + dx) % 4, (yc // 2 + dy) % 4 * 2 + (yc + dc) % 2
                 src = src_of(xd * 8 + ycd)
                 go = functools.partial(

time: 204 us -> 202 us (level)
  no operation moved by 1% of the time
where the time goes in v3:
time: 202 us
  Pallas kernels  198 us (98%)
  local copies, waits for them, and re-layouts  3.5 us (2%)
    pallas_call x1, Pallas kernels, expert_layer(): pl.pallas_call(kernel, name='expert_layer', out_shape=(jax.ShapeDtypeStru...  198 us

profile of v3, /device:TPU:1, one launch (start us, length us, event | category | flops | bytes accessed | tf_op | source)
XLA Modules:
  0.0 202.0 jit_solution(8337774633745393117)
XLA Ops:
  0.6 197.9 %expert_layer.1 = (bf16[1024,512]{1,0:T(8,128)(2,1)}, f32[2,128]{1,0:T(2,128)}) custom-call(s32[2,128]{1,0:T(2,128)} %bitcast.10, f32[2,128]{1,0:T(2,128)} %bitcast.11, bf16[1024,512]{1,0:T(8,128)(2,1)} %tok.1, bf16[1024,512]{1,0:T(8,128)(2,1)} %dy.1, bf16[4096,768]{1,0:T(8,128)(2,1)} %bitcast.7, bf16[4096,768]{1,0:T(8,128)(2,1)} %bitcast.8, ...), custom_call_target="tpu_custom_call" | custom-call | flops 35999997952 | bytes 25000000 | tf_op jit(solution)/shard_map/expert_layer/pallas_call | solution.py:534
  198.5 2.3 %copy.11 = bf16[1024,512]{1,0:T(8,128)(2,1)} copy(bf16[1024,512]{1,0:T(8,128)(2,1)} %get-tuple-element.8) | data formatting | bytes 2097152
  200.8 1.2 copy.12

commit v4 on v3

--- a/solution.py
+++ b/solution.py
@@ -150,10 +150,10 @@
             parts.append(jnp.where(hit, 1.0, 0.0).astype(BF16))
         return jnp.concatenate(parts, axis=1)
 
-    def spread(src_of, dst, s_sem, r_sem_of):
+    def spread(src_of, dst, s_sem, r_sem_of, steps=STEPS):
         def side(n, c):
             dc = 1 - n
-            for dx, dy in STEPS:
+            for dx, dy in steps:
                 xd, ycd = (x + dx) % 4, (yc // 2 + dy) % 4 * 2 + (yc + dc) % 2
                 src = src_of(xd * 8 + ycd)
                 go = functools.partial(
@@ -205,20 +205,26 @@
         wait(buf.at[pl.ds(0, ROWS)], b_s.at[b])
 
     def batch(b, slot, src, zl_src, zl_dst, dst, r_sem_of):
-        def step(i, c):
-            dx = near_first(3 - i)
-            xd = (x + dx) % 4
-            picked = dot(select(zl_src, zl_dst * 4 + xd), src[...])
-            buf[chunk(4 * slot + xd), :] = picked.astype(BF16)
-            if b < 0:
-                spread_at(dx, src_of, dst, b_s.at[b], r_sem_of(dx))
-            return c
+        def gather(first):
+            def step(i, c):
+                xd = (x + first + 2 * i) % 4
+                picked = dot(select(zl_src, zl_dst * 4 + xd), src[...])
+                buf[chunk(4 * slot + xd), :] = picked.astype(BF16)
+                return c
+
+            lax.fori_loop(0, 2, step, 0)
 
         def src_of(k):
             return buf.at[rows(32 * slot + k)]
 
-        lax.fori_loop(0, 4, step, 0)
-        if b >= 0:
+        if b == 0:
+            for first in (0, 1):
+                gather(first)
+                part = [step for step in STEPS if step[0] % 2 == first]
+                spread(src_of, dst, b_s.at[b], r_sem_of, part)
+        else:
+            gather(0)
+            gather(1)
             spread(src_of, dst, b_s.at[b], r_sem_of)
 
     def x_out(b, slot, s):

time: 202 us -> 205 us (1.015)
  Pallas kernels: 198 us -> 201 us
    pallas_call x1, Pallas kernels: 198 us -> 201 us  [expert_layer(): pl.pallas_call(kernel, name='expert_layer', out_shape=(jax.ShapeDtypeStru...]
where the time goes in v4:
time: 205 us
  Pallas kernels  201 us (98%)
  local copies, waits for them, and re-layouts  3.5 us (2%)
    pallas_call x1, Pallas kernels, expert_layer(): pl.pallas_call(kernel, name='expert_layer', out_shape=(jax.ShapeDtypeStru...  201 us

profile of v4, /device:TPU:1, one launch (start us, length us, event | category | flops | bytes accessed | tf_op | source)
XLA Modules:
  0.0 204.7 jit_solution(2283840670838314745)
XLA Ops:
  0.6 200.6 %expert_layer.1 = (bf16[1024,512]{1,0:T(8,128)(2,1)}, f32[2,128]{1,0:T(2,128)}) custom-call(s32[2,128]{1,0:T(2,128)} %bitcast.10, f32[2,128]{1,0:T(2,128)} %bitcast.11, bf16[1024,512]{1,0:T(8,128)(2,1)} %tok.1, bf16[1024,512]{1,0:T(8,128)(2,1)} %dy.1, bf16[4096,768]{1,0:T(8,128)(2,1)} %bitcast.7, bf16[4096,768]{1,0:T(8,128)(2,1)} %bitcast.8, ...), custom_call_target="tpu_custom_call" | custom-call | flops 35999997952 | bytes 25000000 | tf_op jit(solution)/shard_map/expert_layer/pallas_call | solution.py:540
  201.2 2.3 %copy.11 = bf16[1024,512]{1,0:T(8,128)(2,1)} copy(bf16[1024,512]{1,0:T(8,128)(2,1)} %get-tuple-element.8) | data formatting | bytes 2097152
  203.5 1.2 copy.12
